TPU v7x, 512 devices: a whole 4x8x8 slice. The times are simulated.
512 devices in a mesh: img: 16 (over y, core), proj: 32 (over z, x).
Axes of the slice: x: 4, y: 8, z: 8, core: 2. Of those that a mesh axis runs over, the one named last changes fastest.
Arguments:
- images: bfloat16 [2048, 4096], P('img'), may hold values from -48 to 48
- projections: bfloat16 [2560, 4096], P('proj'), may hold values from -6 to 6
- noise_weight: float32 [4096], replicated, may hold values from 0.02 to 0.08
- defocus: float32 [2048], P('img'), may hold values from 2 to 8
- orient_count: int32 [2048], P('img'), may hold values from 160 to 2560, as said below
- term_limit: int32 [2048], P('img'), may hold values from 2048 to 4096
- block_plan: int32 [64], replicated, may hold values from 0 to 63, each once
Outputs:
- reconstruction: bfloat16 [2560, 4096], P('proj', 'img')
- evidence_next: float32 [2048], P('img')
Inputs may be any that keep to these rules, and one draw needn't show every extreme that they name: Orientations 0 to orient_count[i] - 1 are the significant ones of image i; some image has all 2560.
All inputs are finite; a program needn't handle non-finite values.
Results may differ from a plain program's by a relative error of at most 0.018.
Values may be sent and summed in bfloat16 or wider, within the bound.
No kernel may reach another device: no remote copies, remote signals or barrier semaphores. Data moves between devices by JAX's collectives and lax.ppermute only.
A program may use at most 64 MiB of HBM per device.

v0:
```python
import math

import jax
import jax.numpy as jnp
from jax import lax
from jax.sharding import PartitionSpec as P

F = 4096
BLOCK = 32


def sent_to_all(array, axis):
    peers = lax.axis_size(axis)
    return lax.all_to_all(
        jnp.broadcast_to(array[None], (peers, *array.shape)), axis, 0, 0, tiled=True
    )


def gathered_once(array, axis):
    leaves = jax.tree.leaves(array)
    turns = sorted(range(len(leaves)), key=lambda k: -leaves[k].size)
    width = (1, *leaves[turns[0]].shape)[-1]
    lines = [
        jnp.pad(leaves[k].reshape(-1), (0, -leaves[k].size % width)).reshape(-1, width)
        for k in turns
    ]
    both, at, found = (sent_to_all(jnp.concatenate(lines), axis), 0, {})
    for k, line in zip(turns, lines):
        slab = both[:, at : at + len(line)].reshape(len(both), -1)
        found[k] = slab[:, : leaves[k].size].reshape(-1, *leaves[k].shape)
        at += len(line)
    numbers = iter(range(len(leaves)))
    return jax.tree.map(lambda _: found[next(numbers)], array)


def combined_pairwise(pieces, combine):
    while len(jax.tree.leaves(pieces)[0]) > 1:
        pieces = jax.vmap(combine)(
            *(jax.tree.map(lambda part: part[side::2], pieces) for side in (0, 1))
        )
    return jax.tree.map(lambda part: part[0], pieces)


def joined_all(array, axis, combine):
    pieces = gathered_once(array, axis)
    return combined_pairwise(pieces, combine)


def cut_along(array, dim, peers):
    before, after = (array.shape[:dim], array.shape[dim + 1 :])
    return jnp.moveaxis(array.reshape(*before, peers, -1, *after), dim, 0)


def sum_at_owner(array, axis, dim):
    peers = lax.axis_size(axis)
    blocks = lax.all_to_all(cut_along(array, dim, peers), axis, 0, 0, tiled=True)
    return jnp.sum(blocks.astype(jnp.float32), axis=0)


def side_by_side(arrays, axis, dim, along):
    widths = [a.shape[along] for a in arrays]
    both = jnp.concatenate(arrays, axis=along)
    filled = sum_at_owner(both, axis, dim)
    return tuple(jnp.split(filled, [sum(widths[:k]) for k in range(1, len(widths))], axis=along))


def contrast_table(defocus, width):
    frequency = (jnp.arange(width, dtype=jnp.float32) + 1.0) / width
    return jnp.sin(2.0 * math.pi * defocus[:, None] * frequency[None, :] + 0.1)


def image_terms(pixels, noise_weight, defocus, limits):
    width = pixels.shape[1]
    contrast = contrast_table(defocus, width)
    keep_mask = (jnp.arange(width, dtype=jnp.int32)[None, :] < limits[:, None]).astype(jnp.float32)
    values = pixels.astype(jnp.float32)
    weighted = (keep_mask * noise_weight[None, :] * contrast * values).astype(jnp.bfloat16)
    weighted_sq = (keep_mask * noise_weight[None, :] * contrast * contrast).astype(jnp.bfloat16)
    back_images = (keep_mask * contrast * values).astype(jnp.bfloat16)
    return (weighted, weighted_sq, back_images)


def join_mass(first, second):
    joined = jnp.maximum(first[0], second[0])
    total = first[1] * jnp.exp(first[0] - joined) + second[1] * jnp.exp(second[0] - joined)
    return (joined, total)


def shards(images, projections, noise_weight, defocus, orient_count, term_limit, block_plan):
    proj_rows = projections.shape[0]
    img_rows = images.shape[0]
    weighted, weighted_sq, back_images = image_terms(images, noise_weight, defocus, term_limit)
    proj_sq = (projections.astype(jnp.float32) * projections.astype(jnp.float32)).astype(
        jnp.bfloat16
    )
    contract = (((1,), (1,)), ((), ()))
    scores = lax.dot_general(projections, weighted, contract, preferred_element_type=jnp.float32)
    scores = scores - 0.5 * lax.dot_general(
        proj_sq, weighted_sq, contract, preferred_element_type=jnp.float32
    )
    orient_ids = lax.axis_index("proj") * proj_rows + jnp.arange(proj_rows, dtype=jnp.int32)
    significant = orient_ids[:, None] < orient_count[None, :]
    local_peak = jnp.max(jnp.where(significant, scores, -1e30), axis=0)
    safe = jnp.where(significant, scores, local_peak[None, :])
    local_mass = jnp.sum(jnp.where(significant, jnp.exp(safe - local_peak[None, :]), 0.0), axis=0)
    row_peak, row_mass = joined_all((local_peak, local_mass), "proj", join_mass)
    log_evidence = row_peak + jnp.log(row_mass)
    posterior = jnp.where(significant, jnp.exp(scores - log_evidence[None, :]), 0.0).astype(
        jnp.bfloat16
    )
    contrast = contrast_table(defocus, F)
    keep_mask = (jnp.arange(F, dtype=jnp.int32)[None, :] < term_limit[:, None]).astype(jnp.float32)
    back_weights = (keep_mask * contrast * contrast).astype(jnp.bfloat16)
    part_images = jnp.dot(posterior, back_images, preferred_element_type=jnp.float32)
    part_weights = jnp.dot(posterior, back_weights, preferred_element_type=jnp.float32)
    sum_images, sum_weights = side_by_side(
        (part_images.astype(jnp.bfloat16), part_weights.astype(jnp.bfloat16)), "img", 1, 0
    )
    reconstruction = (sum_images / (sum_weights + 1.0)).astype(jnp.bfloat16)
    every_evidence = lax.all_gather(log_evidence, "img", axis=0, tiled=True)
    blocks = every_evidence.reshape(-1, BLOCK)
    local_blocks = img_rows // BLOCK
    slot_ids = lax.axis_index("img") * local_blocks + jnp.arange(local_blocks, dtype=jnp.int32)
    selector = (block_plan[None, :] == slot_ids[:, None]).astype(jnp.float32)
    own_blocks = jnp.dot(selector, blocks, precision=lax.Precision.HIGHEST)
    return (reconstruction, own_blocks.reshape(img_rows))


def solution(mesh):
    placed = (P("img", None), P("proj", None), P(), P("img"), P("img"), P("img"), P())
    return jax.shard_map(
        shards, mesh=mesh, in_specs=placed, out_specs=(P("proj", "img"), P("img")), check_vma=False
    )
```

profile of v0, /device:TPU:1, one launch (start us, length us, event | category | flops | bytes accessed | tf_op | source)
XLA Modules:
  0.0 112.6 jit_solution(15977206153363226754)
XLA Ops:
  0.7 0.7 broadcast_multiply_fusion
  1.3 0.0 copy-start
  1.3 0.0 copy-start.2
  1.3 0.0 copy-start.3
  1.3 0.0 copy-start.4
  1.3 9.5 %convolution_bitcast_fusion = f32[80,128]{1,0:T(8,128)S(1)} fusion(bf16[80,4096]{1,0:T(8,128)(2,1)} %param.8, bf16[128,4096]{1,0:T(8,128)(2,1)} %param.7, f32[4096]{0:T(1024)S(1)} %add_multiply_fusion, f32[128]{0:T(128)S(1)} %broadcast_multiply_fusion, f32[4096]{0:T(1024)} %param.9, s32[128]{0:T(128)} %param.12), kind=kOutput, calls=%fused_computation.18 | convolution fusion | flops 88080384 | bytes 1778688 | tf_op jit(solution)/shard_map/dot_general | solution.py:97
  10.8 0.0 copy-done
  10.8 0.0 copy-done.2
  10.9 0.0 copy-done.3
  10.9 0.0 copy-done.4
  10.9 7.8 %fusion.30 = (f32[128]{0:T(128)S(1)}, f32[80,128]{1,0:T(8,128)S(1)}) fusion(s32[128]{0:T(128)S(1)} %copy-done, s32[80]{0:T(128)S(1)} %iota_add_fusion.1, f32[80,128]{1,0:T(8,128)S(1)} %convolution_bitcast_fusion, f32[4096]{0:T(1024)S(1)} %add_multiply_fusion, f32[128]{0:T(128)S(1)} %broadcast_multiply_fusion, f32[4096]{0:T(1024)S(1)} %copy-done.3, ...), kind=kOutput, calls=%fused_computation.46 | convolution fusion | flops 88590208 | bytes 772416 | tf_op jit(solution)/shard_map/dot_general | solution.py:98
  18.7 0.1 fusion.33
  18.9 22.2 %all_to_all.10 = f32[32,2,128]{2,1,0:T(2,128)S(1)} all-to-all(f32[32,2,128]{2,1,0:T(2,128)S(1)} %broadcast_in_dim.21), channel_id=1, replica_groups=mesh['img'=16,'proj'=32] {'proj'}, dimensions={0} | all-to-all | bytes 65536 | tf_op jit(solution)/shard_map/all_to_all | solution.py:14
  41.5 0.0 copy-start.1
  41.5 7.4 %convolution_convert_fusion = bf16[80,4096]{1,0:T(8,128)(2,1)S(1)} fusion(f32[4096]{0:T(1024)S(1)} %add_multiply_fusion, f32[128]{0:T(128)S(1)} %broadcast_multiply_fusion, s32[128]{0:T(128)S(1)} %copy-done.4, f32[80,128]{1,0:T(8,128)S(1)} %get-tuple-element.13, f32[128]{0:T(128)S(1)} %bitcast.25, s32[128]{0:T(128)S(1)} %copy-done, s32[80]{0:T(128)S(1)} %iota_add_fusion.1), kind=kOutput, calls=%fused_computation | convolution fusion | flops 87400448 | bytes 715072 | tf_op jit(solution)/shard_map/dot_general | solution.py:115
  48.9 0.0 copy-done.1
  48.9 7.8 %convolution_convert_fusion.1 = bf16[80,4096]{1,0:T(8,128)(2,1)S(1)} fusion(bf16[128,4096]{1,0:T(8,128)(2,1)S(1)} %copy-done.1, f32[4096]{0:T(1024)S(1)} %add_multiply_fusion, f32[128]{0:T(128)S(1)} %broadcast_multiply_fusion, s32[128]{0:T(128)S(1)} %copy-done.4, f32[80,128]{1,0:T(8,128)S(1)} %get-tuple-element.13, f32[128]{0:T(128)S(1)} %bitcast.26, ...), kind=kOutput, calls=%fused_computation.1 | convolution fusion | flops 87924736 | bytes 1763648 | tf_op jit(solution)/shard_map/dot_general | solution.py:114
  56.7 0.1 pad_maximum_fusion
  56.8 1.2 %copy.14 = bf16[20,16,8,256]{3,2,0,1:T(8,128)(2,1)} copy(bf16[20,16,8,256]{3,2,1,0:T(8,128)(2,1)S(1)} %bitcast.18) | data formatting | bytes 2621440 | tf_op jit(solution)/shard_map/reshape | solution.py:51
  58.0 0.0 copy-start.5
  58.0 9.3 %all-to-all-start.1 = ((bf16[16,160,256]{2,1,0:T(8,128)(2,1)}), bf16[16,160,256]{2,1,0:T(8,128)(2,1)S(1)}, u32[]{:S(2)}, u32[]{:S(2)}) async-start(bf16[16,160,256]{2,1,0:T(8,128)(2,1)} %bitcast.17), calls=%async_computation.1 | async-start | bytes 2621440 | tf_op jit(solution)/shard_map/all_to_all | solution.py:56
  67.4 42.3 %all-gather = f32[1,2048]{1,0:T(1,128)S(1)} all-gather(f32[1,128]{1,0:T(1,128)S(1)} %log_add_fusion), channel_id=2, replica_groups=mesh['img'=16,'proj'=32] {'img'}, dimensions={1}, use_global_device_ids=true | all-gather | bytes 8704 | tf_op jit(solution)/shard_map/all_gather | solution.py:120
  109.7 0.5 broadcast.80
  110.2 0.7 reduce.3
  110.9 0.1 reshape.53
  110.9 0.0 copy-done.5
  110.9 0.2 fusion.35
  111.1 0.6 reshape.54
  111.7 0.0 all-to-all-done.1
  111.7 0.2 convert_reduce_fusion
  111.9 0.6 fusion.29
  (27 shorter events, 0.4 us)
Async XLA Ops:
  1.3 9.5 %copy-start = (s32[128]{0:T(128)S(1)}, s32[128]{0:T(128)}, u32[]{:S(2)}) copy-start(s32[128]{0:T(128)} %param.11) | copy-start | bytes 1540
  1.3 9.5 %copy-start.2 = (bf16[80,4096]{1,0:T(8,128)(2,1)S(1)}, bf16[80,4096]{1,0:T(8,128)(2,1)}, u32[]{:S(2)}) copy-start(bf16[80,4096]{1,0:T(8,128)(2,1)} %param.8) | copy-start | bytes 1966084
  1.3 9.5 %copy-start.3 = (f32[4096]{0:T(1024)S(1)}, f32[4096]{0:T(1024)}, u32[]{:S(2)}) copy-start(f32[4096]{0:T(1024)} %param.9) | copy-start | bytes 49156
  1.3 9.5 %copy-start.4 = (s32[128]{0:T(128)S(1)}, s32[128]{0:T(128)}, u32[]{:S(2)}) copy-start(s32[128]{0:T(128)} %param.12) | copy-start | bytes 1540
  41.5 7.5 %copy-start.1 = (bf16[128,4096]{1,0:T(8,128)(2,1)S(1)}, bf16[128,4096]{1,0:T(8,128)(2,1)}, u32[]{:S(2)}) copy-start(bf16[128,4096]{1,0:T(8,128)(2,1)} %param.7) | copy-start | bytes 3145732
  58.0 52.9 %copy-start.5 = (s32[64]{0:T(128)S(1)}, s32[64]{0:T(128)}, u32[]{:S(2)}) copy-start(s32[64]{0:T(128)} %param.13) | copy-start | bytes 772
  58.0 53.7 %all-to-all-start.1 = ((bf16[16,160,256]{2,1,0:T(8,128)(2,1)}), bf16[16,160,256]{2,1,0:T(8,128)(2,1)S(1)}, u32[]{:S(2)}, u32[]{:S(2)}) async-start(bf16[16,160,256]{2,1,0:T(8,128)(2,1)} %bitcast.17), calls=%async_computation.1 | async-start | bytes 2621440 | tf_op jit(solution)/shard_map/all_to_all | solution.py:56
where the time goes:
time: 113 us
  blocking collectives  64.5 us (57%)
  matrix products  32.7 us (29%)
  starting transfers between devices  9.35 us (8%)
  local copies, waits for them, and re-layouts  2.71 us (2%)
  other arithmetic  2.46 us (2%)
    all_gather x1, blocking collectives, shards(): every_evidence = lax.all_gather(log_evidence, 'img', axis=0, tiled=True)  42.3 us
    all_to_all x1, blocking collectives, sent_to_all(): lax.all_to_all(jnp.broadcast_to(array[None], (peers, *array.shape)), axis...  22.2 us
    dot_general x1, matrix products, shards(): lax.dot_general(projections, weighted, contract, preferred_element_type=j...  9.5 us
    all_to_all x1, starting transfers between devices, sum_at_owner(): lax.all_to_all(cut_along(array, dim, peers), axis, 0, 0, tiled=True)  9.35 us
    dot_general x1, matrix products, shards(): lax.dot_general(proj_sq, weighted_sq, contract, preferred_element_type=jn...  7.83 us
    dot_general x1, matrix products, shards(): jnp.dot(posterior, back_images, preferred_element_type=jnp.float32)  7.77 us
    dot_general x1, matrix products, shards(): jnp.dot(posterior, back_weights, preferred_element_type=jnp.float32)  7.44 us
  transfers between devices with their start and end apart: 1, of which 0 were waited for; matrix products, arithmetic and copies ran while one was open for 2% of the time, Pallas kernels for 0%

commit v1 on v0

v1 whole, which is shorter than its diff:
```python
import functools
import math

import jax
import jax.numpy as jnp
from jax import lax
from jax.experimental import pallas as pl
from jax.experimental.pallas import tpu as pltpu
from jax.sharding import PartitionSpec as P

F = 4096
BLOCK = 32
LANES = 128
COLS = 256
PAD = 16
BF = jnp.bfloat16
F32 = jnp.float32


def small_sin_cos(x):
    y = x * x
    s = 1.0
    for k in (12, 10, 8, 6, 4, 2):
        s = 1.0 - y * s * (1.0 / (k * (k + 1)))
    c = 1.0
    for k in (14, 12, 10, 8, 6, 4, 2):
        c = 1.0 - y * c * (1.0 / (k * (k - 1)))
    return x * s, c


def down_rows(row):
    n = row.shape[1]
    return jnp.transpose(jnp.broadcast_to(row, (n, n)))


def score_kernel(pixels, proj, noise, defocus, counts, limits, scores, stats, back, terms, terms_sq, turn, edge):
    rows, images = proj.shape[0], pixels.shape[0]
    lane = lax.broadcasted_iota(jnp.int32, (images, LANES), 1).astype(F32)
    angle = down_rows(defocus[...]) * ((lane + 1.0) * (2.0 * math.pi / F))
    base_s, base_c = small_sin_cos(angle)
    turn[0] = base_s * math.cos(0.1) + base_c * math.sin(0.1)
    turn[1] = base_c * math.cos(0.1) - base_s * math.sin(0.1)
    turn[2] = jnp.broadcast_to(base_s[:, LANES - 1 :], (images, LANES))
    turn[3] = jnp.broadcast_to(base_c[:, LANES - 1 :], (images, LANES))
    edge[...] = down_rows(limits[...].astype(F32)) - lane

    total = jnp.zeros((rows, images), F32)
    total_sq = jnp.zeros((rows, images), F32)
    contract = (((1,), (1,)), ((), ()))
    steps = COLS // LANES
    for g in range(F // COLS):
        for r in range(0, images, 16):
            some = slice(r, r + 16)
            s, c = turn[0, some], turn[1, some]
            step_s, step_c = turn[2, some], turn[3, some]
            last = edge[some]
            for h in range(steps):
                t = g * steps + h
                at = slice(t * LANES, (t + 1) * LANES)
                inner = slice(h * LANES, (h + 1) * LANES)
                kept = jnp.where(last > float(t * LANES), s, 0.0)
                image = kept * pixels[some, at].astype(F32)
                square = kept * s
                weight = noise[:, at]
                back[g, 0, some, inner] = image.astype(BF)
                back[g, 1, some, inner] = square.astype(BF)
                terms[some, at] = (weight * image).astype(BF)
                terms_sq[some, at] = (weight * square).astype(BF)
                s, c = s * step_c + c * step_s, c * step_c - s * step_s
            turn[0, some], turn[1, some] = s, c
        at = slice(g * COLS, (g + 1) * COLS)
        some_proj = proj[:, at]
        wide = some_proj.astype(F32)
        total += lax.dot_general(some_proj, terms[:, at], contract, preferred_element_type=F32)
        total_sq += lax.dot_general((wide * wide).astype(BF), terms_sq[:, at], contract, preferred_element_type=F32)
    found = total - 0.5 * total_sq
    orient = lax.axis_index("proj") * rows + lax.broadcasted_iota(jnp.int32, (rows, images), 0)
    significant = orient < counts[...]
    found = jnp.where(significant, found, -1e30)
    peak = jnp.max(found, axis=0, keepdims=True)
    mass = jnp.sum(jnp.where(significant, jnp.exp(found - peak), 0.0), axis=0, keepdims=True)
    scores[...] = found
    both = jnp.concatenate([peak, mass], axis=0)
    stats[...] = jnp.broadcast_to(both[None], stats.shape)


def thirds(x):
    first = x.astype(BF)
    rest = x - first.astype(F32)
    second = rest.astype(BF)
    return first, second, (rest - second.astype(F32)).astype(BF)


def back_kernel(scores, stats, back, counts, own, other):
    rows, images = scores.shape
    peaks, masses = stats[:, 0, :], stats[:, 1, :]
    peak = jnp.max(peaks, axis=0, keepdims=True)
    mass = jnp.sum(masses * jnp.exp(peaks - peak), axis=0, keepdims=True)
    evidence = peak + jnp.log(mass)
    orient = lax.axis_index("proj") * rows + lax.broadcasted_iota(jnp.int32, (rows, images), 0)
    significant = orient < counts[...]
    posterior = jnp.where(significant, jnp.exp(scores[...] - evidence), 0.0).astype(BF)
    core = lax.rem(lax.axis_index("img"), 2)
    here = lax.broadcasted_iota(jnp.int32, (PAD, COLS), 1) // LANES == core
    line = lax.broadcasted_iota(jnp.int32, (PAD, COLS), 0)
    wide = jnp.concatenate([evidence, evidence], axis=1)
    note = jnp.zeros((PAD, COLS), F32)
    for k, part in enumerate(thirds(wide)):
        note = jnp.where(line == k, part.astype(F32), note)
    note = jnp.where(here, note, 0.0).astype(BF)
    for out, side in ((own, core), (other, 1 - core)):
        for y in range(own.shape[0]):
            for k in range(2):
                part = jnp.dot(posterior, back[2 * y + side, k], preferred_element_type=F32)
                out[y, k * rows : (k + 1) * rows, :] = part.astype(BF)
            out[y, 2 * rows :, :] = note


def last_kernel(parts, plan, reconstruction, evidence):
    rows = reconstruction.shape[0]
    chips = parts.shape[0]
    images = parts[0, :rows, :].astype(F32)
    weights = parts[0, rows : 2 * rows, :].astype(F32)
    for y in range(1, chips):
        images += parts[y, :rows, :].astype(F32)
        weights += parts[y, rows : 2 * rows, :].astype(F32)
    reconstruction[...] = (images / (weights + 1.0)).astype(BF)
    lines = []
    for y in range(chips):
        note = parts[y, 2 * rows :, :].astype(F32)
        full = (note[0:1] + note[1:2]) + note[2:3]
        lines += [full[:, :LANES], full[:, LANES:]]
    known = jnp.concatenate(lines, axis=0)
    line = lax.broadcasted_iota(jnp.int32, known.shape, 0)
    group = lax.broadcasted_iota(jnp.int32, known.shape, 1) // BLOCK
    per_line = LANES // BLOCK
    number = line * per_line + group
    target = jnp.zeros(known.shape, jnp.int32)
    for b in range(2 * chips * per_line):
        target = jnp.where(number == b, plan[b], target)
    slot = lax.axis_index("img") * per_line + group
    placed = jnp.zeros((1, LANES), F32)
    for k in range(per_line):
        moved = known if k == 0 else pltpu.roll(known, k * BLOCK, 1)
        goal = target if k == 0 else pltpu.roll(target, k * BLOCK, 1)
        placed += jnp.sum(jnp.where(goal == slot, moved, 0.0), axis=0, keepdims=True)
    evidence[...] = placed


def vmem(n):
    return [pl.BlockSpec(memory_space=pltpu.VMEM)] * n


def shards(images, projections, noise_weight, defocus, orient_count, term_limit, block_plan):
    rows, count = projections.shape[0], images.shape[0]
    devices, peers = lax.axis_size("img"), lax.axis_size("proj")
    chips = devices // 2
    limit = pltpu.CompilerParams(vmem_limit_bytes=48 * 2**20)
    counts = orient_count.reshape(1, count)
    scores, stats, back = pl.pallas_call(
        score_kernel,
        name="score",
        out_shape=(
            jax.ShapeDtypeStruct((rows, count), F32),
            jax.ShapeDtypeStruct((peers, 2, count), F32),
            jax.ShapeDtypeStruct((devices, 2, count, COLS), BF),
        ),
        in_specs=vmem(6),
        out_specs=tuple(vmem(3)),
        scratch_shapes=[
            pltpu.VMEM((count, F), BF),
            pltpu.VMEM((count, F), BF),
            pltpu.VMEM((4, count, LANES), F32),
            pltpu.VMEM((count, LANES), F32),
        ],
        compiler_params=limit,
    )(
        images,
        projections,
        noise_weight.reshape(1, F),
        defocus.reshape(1, count),
        counts,
        term_limit.reshape(1, count),
    )
    stats = lax.all_to_all(stats, "proj", 0, 0, tiled=True)
    shape = jax.ShapeDtypeStruct((chips, 2 * rows + PAD, COLS), BF)
    own, other = pl.pallas_call(
        back_kernel,
        name="back",
        out_shape=(shape, shape),
        in_specs=vmem(4),
        out_specs=tuple(vmem(2)),
        compiler_params=limit,
    )(scores, stats, back, counts)
    other = lax.ppermute(other, "img", [(i, i ^ 1) for i in range(devices)])
    both = (own.astype(F32) + other.astype(F32)).astype(BF)
    same_core = [[2 * y + c for y in range(chips)] for c in range(2)]
    parts = lax.all_to_all(both, "img", 0, 0, tiled=True, axis_index_groups=same_core)
    reconstruction, evidence = pl.pallas_call(
        last_kernel,
        name="last",
        out_shape=(
            jax.ShapeDtypeStruct((rows, COLS), BF),
            jax.ShapeDtypeStruct((1, count), F32),
        ),
        in_specs=[*vmem(1), pl.BlockSpec(memory_space=pltpu.SMEM)],
        out_specs=tuple(vmem(2)),
        compiler_params=limit,
    )(parts, block_plan)
    return reconstruction, evidence.reshape(count)


def solution(mesh):
    placed = (P("img", None), P("proj", None), P(), P("img"), P("img"), P("img"), P())
    return jax.shard_map(
        shards, mesh=mesh, in_specs=placed, out_specs=(P("proj", "img"), P("img")), check_vma=False
    )
```

time: 113 us -> 65.8 us (0.58)
  matrix products: 32.7 us -> 0 us
  blocking collectives: 64.5 us -> 49.7 us
  starting transfers between devices: 9.35 us -> 4.01 us
  Pallas kernels: 0 us -> 4.04 us
  local copies, waits for them, and re-layouts: 2.71 us -> 4.99 us
  other arithmetic: 2.46 us -> 0.2 us
  waiting for transfers between devices: 0.01 us -> 1.8 us
    all_gather x1 -> x0, blocking collectives: 42.3 us -> none  [shards(): every_evidence = lax.all_gather(log_evidence, 'img', axis=0, tiled=True)]
    dot_general x5 -> x0, matrix products: 32.7 us -> none  [the longest x1 9.5 us: shards(): lax.dot_general(projections, weighted, contract, preferred_element_type=j...]
    all_to_all x1 -> x2, blocking collectives: 22.2 us -> 49.7 us  [the longest x1 27.5 us: shards(): lax.all_to_all(both, 'img', 0, 0, tiled=True, axis_index_groups=same_core)]
    all_to_all x1 -> x0, starting transfers between devices: 9.35 us -> none  [sum_at_owner(): lax.all_to_all(cut_along(array, dim, peers), axis, 0, 0, tiled=True)]
    unnamed x12 -> x14, local copies, waits for them, and re-layouts: 0.02 us -> 4.99 us
    pallas_call x0 -> x3, Pallas kernels: none -> 4.04 us  [the longest x1 2.17 us: shards(): pl.pallas_call(score_kernel, name='score', out_shape=(jax.ShapeDtypeStruc...]
    ppermute x0 -> x1, starting transfers between devices: none -> 4.01 us  [shards(): other = lax.ppermute(other, 'img', [(i, i ^ 1) for i in range(devices)])]
    reshape x3 -> x0, local copies, waits for them, and re-layouts: 1.89 us -> none  [the longest x1 1.2 us: cut_along(): return jnp.moveaxis(array.reshape(*before, peers, -1, *after), dim, 0)]
  transfers between devices with their start and end apart: 1 -> 1, of which waited for: 0 -> 1; matrix products, arithmetic and copies ran while one was open for 2% -> 0% of each run, Pallas kernels for 0% -> 0%
where the time goes in v1:
time: 65.8 us; the launch traced here: 65.4 us
  blocking collectives  49.7 us (76%)
  local copies, waits for them, and re-layouts  4.99 us (8%)
  Pallas kernels  4.04 us (6%)
  starting transfers between devices  4.01 us (6%)
  waiting for transfers between devices  1.8 us (3%)
  between operations  0.67 us (1%)
    all_to_all x1, blocking collectives, shards(): lax.all_to_all(both, 'img', 0, 0, tiled=True, axis_index_groups=same_core)  27.5 us
    all_to_all x1, blocking collectives, shards(): stats = lax.all_to_all(stats, 'proj', 0, 0, tiled=True)  22.2 us
    unnamed x14, local copies, waits for them, and re-layouts  4.99 us
    ppermute x1, starting transfers between devices, shards(): other = lax.ppermute(other, 'img', [(i, i ^ 1) for i in range(devices)])  4.01 us
    pallas_call x1, Pallas kernels, shards(): pl.pallas_call(score_kernel, name='score', out_shape=(jax.ShapeDtypeStruc...  2.17 us
    ppermute x1, waiting for transfers between devices, shards(): other = lax.ppermute(other, 'img', [(i, i ^ 1) for i in range(devices)])  1.8 us
    pallas_call x1, Pallas kernels, shards(): pl.pallas_call(last_kernel, name='last', out_shape=(jax.ShapeDtypeStruct(...  1.33 us
  transfers between devices with their start and end apart: 1, of which 1 were waited for; matrix products, arithmetic and copies ran while one was open for 0% of the time, Pallas kernels for 0%

profile of v1, /device:TPU:1, one launch (start us, length us, event | category | flops | bytes accessed | tf_op | source)
XLA Modules:
  0.0 65.4 jit_solution(12489083316157072998)
XLA Ops:
  0.6 0.0 copy-start
  0.6 1.2 %copy-done = bf16[128,4096]{1,0:T(8,128)(2,1)S(1)} copy-done((bf16[128,4096]{1,0:T(8,128)(2,1)S(1)}, bf16[128,4096]{1,0:T(8,128)(2,1)}, u32[]{:S(2)}) %copy-start) | copy-done | bytes 1048600
  1.9 0.0 copy-start.1
  1.9 1.1 %copy-done.1 = bf16[80,4096]{1,0:T(8,128)(2,1)S(1)} copy-done((bf16[80,4096]{1,0:T(8,128)(2,1)S(1)}, bf16[80,4096]{1,0:T(8,128)(2,1)}, u32[]{:S(2)}) %copy-start.1) | copy-done | bytes 655384
  2.9 0.0 copy-start.2
  2.9 0.7 %copy-done.2 = f32[4096]{0:T(1024)S(1)} copy-done((f32[4096]{0:T(1024)S(1)}, f32[4096]{0:T(1024)}, u32[]{:S(2)}) %copy-start.2) | copy-done | bytes 16408
  3.7 0.0 copy-start.3
  3.7 0.7 copy-done.3
  4.3 0.0 copy-start.4
  4.3 0.7 copy-done.4
  5.0 0.0 copy-start.5
  5.0 0.7 copy-done.5
  5.6 2.2 %score.1 = (f32[80,128]{1,0:T(8,128)S(1)}, f32[32,2,128]{2,1,0:T(2,128)S(1)}, bf16[16,2,128,256]{3,2,1,0:T(8,128)(2,1)S(1)}) custom-call(bf16[128,4096]{1,0:T(8,128)(2,1)S(1)} %copy-done, bf16[80,4096]{1,0:T(8,128)(2,1)S(1)} %copy-done.1, f32[1,4096]{1,0:T(1,128)S(1)} %bitcast.5, f32[1,128]{1,0:T(1,128)S(1)} %bitcast.8, s32[1,128]{1,0:T(1,128)S(1)} %bitcast.6, ...), custom_call_target="tpu_custom_call" | custom-call | tf_op jit(solution)/shard_map/score/pallas_call | solution.py:160
  7.8 22.2 %all_to_all.10.stats = f32[32,2,128]{2,1,0:T(2,128)S(1)} all-to-all(f32[32,2,128]{2,1,0:T(2,128)S(1)} %get-tuple-element.10), channel_id=1, replica_groups=mesh['img'=16,'proj'=32] {'proj'}, dimensions={0} | all-to-all | bytes 65536 | tf_op jit(solution)/shard_map/all_to_all | solution.py:185
  30.0 0.5 back.1
  30.6 4.0 %collective-permute-start = (bf16[8,176,256]{2,1,0:T(8,128)(2,1)S(1)}, bf16[8,176,256]{2,1,0:T(8,128)(2,1)S(1)}, u32[]{:S(2)}, u32[]{:S(2)}) collective-permute-start(bf16[8,176,256]{2,1,0:T(8,128)(2,1)S(1)} %get-tuple-element.13), channel_id=1, source_target_pairs={{0,32},{32,0},{64,96},{96,64},{128,160},{160,128},{192,224},{224,1... | collective-permute-start | bytes 2162696 | tf_op jit(solution)/shard_map/ppermute | solution.py:195
  34.6 1.8 %collective-permute-done = bf16[8,176,256]{2,1,0:T(8,128)(2,1)S(1)} collective-permute-done((bf16[8,176,256]{2,1,0:T(8,128)(2,1)S(1)}, bf16[8,176,256]{2,1,0:T(8,128)(2,1)S(1)}, u32[]{:S(2)}, u32[]{:S(2)}) %collective-permute-start) | collective-permute-done | bytes 720928 | tf_op jit(solution)/shard_map/ppermute | solution.py:195
  36.4 0.0 copy-start.6
  36.4 0.2 add_convert_fusion
  36.6 27.5 %all_to_all.11.parts = bf16[8,176,256]{2,1,0:T(8,128)(2,1)S(1)} all-to-all(bf16[8,176,256]{2,1,0:T(8,128)(2,1)S(1)} %add_convert_fusion), channel_id=1, replica_groups={{0,64,128,192,256,320,384,448},{32,96,160,224,288,352,416,480},{1,65,12..., dimensions={0} | all-to-all | bytes 1441792 | tf_op jit(solution)/shard_map/all_to_all | solution.py:198
  64.1 0.0 copy-done.6
  64.1 1.3 %last.1 = (bf16[80,256]{1,0:T(8,128)(2,1)}, f32[1,128]{1,0:T(1,128)}) custom-call(bf16[8,176,256]{2,1,0:T(8,128)(2,1)S(1)} %all_to_all.11.parts, s32[64]{0:T(128)S(1)} %copy-done.6), custom_call_target="tpu_custom_call" | custom-call | tf_op jit(solution)/shard_map/last/pallas_call | solution.py:199
Async XLA Ops:
  0.6 1.2 %copy-start = (bf16[128,4096]{1,0:T(8,128)(2,1)S(1)}, bf16[128,4096]{1,0:T(8,128)(2,1)}, u32[]{:S(2)}) copy-start(bf16[128,4096]{1,0:T(8,128)(2,1)} %pixels.1) | copy-start | bytes 3145732
  1.9 1.1 %copy-start.1 = (bf16[80,4096]{1,0:T(8,128)(2,1)S(1)}, bf16[80,4096]{1,0:T(8,128)(2,1)}, u32[]{:S(2)}) copy-start(bf16[80,4096]{1,0:T(8,128)(2,1)} %proj.1) | copy-start | bytes 1966084
  2.9 0.7 %copy-start.2 = (f32[4096]{0:T(1024)S(1)}, f32[4096]{0:T(1024)}, u32[]{:S(2)}) copy-start(f32[4096]{0:T(1024)} %param.9) | copy-start | bytes 49156
  3.7 0.7 %copy-start.3 = (s32[128]{0:T(128)S(1)}, s32[128]{0:T(128)}, u32[]{:S(2)}) copy-start(s32[128]{0:T(128)} %param.11) | copy-start | bytes 1540
  4.3 0.7 %copy-start.4 = (f32[128]{0:T(128)S(1)}, f32[128]{0:T(128)}, u32[]{:S(2)}) copy-start(f32[128]{0:T(128)} %param.10) | copy-start | bytes 1540
  5.0 0.7 %copy-start.5 = (s32[128]{0:T(128)S(1)}, s32[128]{0:T(128)}, u32[]{:S(2)}) copy-start(s32[128]{0:T(128)} %param.12) | copy-start | bytes 1540
  30.6 5.8 %collective-permute-start = (bf16[8,176,256]{2,1,0:T(8,128)(2,1)S(1)}, bf16[8,176,256]{2,1,0:T(8,128)(2,1)S(1)}, u32[]{:S(2)}, u32[]{:S(2)}) collective-permute-start(bf16[8,176,256]{2,1,0:T(8,128)(2,1)S(1)} %get-tuple-element.13), channel_id=1, source_target_pairs={{0,32},{32,0},{64,96},{96,64},{128,160},{160,128},{192,224},{224,1... | collective-permute-start | bytes 2162696 | tf_op jit(solution)/shard_map/ppermute | solution.py:195
  36.4 27.7 %copy-start.6 = (s32[64]{0:T(128)S(1)}, s32[64]{0:T(128)}, u32[]{:S(2)}) copy-start(s32[64]{0:T(128)} %plan.1) | copy-start | bytes 772
